TPU v7x, 32 devices: a whole 2x2x4 slice. The times are simulated.
32 devices in a mesh: dp: 4 (over y, core), expert: 8 (over z, x).
Axes of the slice: x: 2, y: 2, z: 4, core: 2. Of those that a mesh axis runs over, the one named last changes fastest.
Arguments:
- tokens: bfloat16 [12608, 512], P(('dp', 'expert')), may hold values from -6 to 6
- w_qkv: bfloat16 [512, 1536], P('dp', 'expert'), may hold values from -1 to 1
- w_out: bfloat16 [512, 512], P('dp', 'expert'), may hold values from -2 to 2
- w_router: bfloat16 [512, 8], P('dp', 'expert'), may hold values from -0.1875 to 0.1875
- norm_params: bfloat16 [4, 512], P(None, 'expert'), may hold values from -1 to 2
- w_in: bfloat16 [8, 512, 2048], P('expert', None, 'dp'), may hold values from -0.25 to 0.25
- w_down: bfloat16 [8, 2048, 512], P('expert', 'dp'), may hold values from -6 to 6
- routes: int32 [12608, 2], P(('dp', 'expert')), may hold values from 0 to 7, all different within a row; in each aligned block of 394 rows (0 to 393, 394 to 787, ...) at most 184 rows name the same one
- threshold: int32 [1], replicated, may hold values from 1 to 4
- cotangent: bfloat16 [12608, 512], P(('dp', 'expert')), may hold values from -6 to 6
Outputs:
- block_out: bfloat16 [12608, 512], P(('dp', 'expert'))
- grad_tokens: bfloat16 [12608, 512], P(('dp', 'expert'))
- grad_qkv: float32 [512, 1536], P('dp', 'expert')
- grad_out: float32 [512, 512], P('dp', 'expert')
- grad_router: float32 [512, 8], P('dp', 'expert')
- grad_norms: float32 [4, 512], P(None, 'expert')
- grad_in: float32 [8, 512, 2048], P('expert', None, 'dp')
- grad_down: float32 [8, 2048, 512], P('expert', 'dp')
- clipped_qkv: float32 [512, 1536], P('dp', 'expert')
- clip_factors: float32 [8], replicated
Inputs may be any that keep to these rules, and one draw needn't show every extreme that they name: `routes`: each token names 2 different experts; in the rows of one device no expert is named by more than 184 rows, a bound that some block reaches there.
All inputs are finite; a program needn't handle non-finite values.
Results may differ from a plain program's by a relative error of at most 0.023.
Values may be sent and summed in bfloat16 or wider, within the bound.
A program may use at most 128 MiB of HBM per device.

v0:
```python
import jax
import jax.numpy as jnp
from jax import lax
from jax.sharding import PartitionSpec as P

D = 512
HEADS = 8
HEAD = 64
SEQ = 197


EPS = 1e-06
LEARN = 0.001


def layer_norm(values, norm_gain, norm_shift):
    center = jnp.mean(values, axis=-1, keepdims=True)
    centered = values - center
    inverse = lax.rsqrt(jnp.mean(centered * centered, axis=-1, keepdims=True) + EPS)
    normed = centered * inverse
    return (normed * norm_gain + norm_shift, normed, inverse)


def norm_back(upstream, normed, inverse, norm_gain):
    scaled = upstream * norm_gain
    inner_term = (
        scaled
        - jnp.mean(scaled, axis=-1, keepdims=True)
        - normed * jnp.mean(scaled * normed, axis=-1, keepdims=True)
    )
    return (inverse * inner_term, jnp.sum(upstream * normed, axis=0), jnp.sum(upstream, axis=0))


def exact_gelu(inputs):
    return jax.nn.gelu(inputs, approximate=False)


def scores_of(queries, key_part):
    return jnp.einsum(
        "bqhd,bkhd->bhqk", queries, key_part, preferred_element_type=jnp.float32
    ) * HEAD ** (-0.5)


def contract_rows(left, right):
    return lax.dot_general(
        left, right, (((0,), (0,)), ((), ())), preferred_element_type=jnp.float32
    )


def contract_cols(left, right):
    return lax.dot_general(
        left, right, (((1,), (1,)), ((), ())), preferred_element_type=jnp.float32
    )


def fetch_forward(w_qkv, w_out, w_router, norm_params, w_in, w_down):
    col_parts = (
        lax.all_gather(w_qkv, "expert", axis=1, tiled=True),
        lax.all_gather(w_out, "expert", axis=1, tiled=True),
        lax.all_gather(w_router, "expert", axis=1, tiled=True),
        lax.all_gather(norm_params, "expert", axis=1, tiled=True),
    )
    full_parts = (
        lax.all_gather(col_parts[0], "dp", axis=0, tiled=True),
        lax.all_gather(col_parts[1], "dp", axis=0, tiled=True),
        lax.all_gather(col_parts[2], "dp", axis=0, tiled=True),
        lax.all_gather(w_in, "dp", axis=2, tiled=True),
        lax.all_gather(w_down, "dp", axis=1, tiled=True),
    )
    return (full_parts, col_parts[3])


def fetch_backward(w_qkv, w_out, w_router, w_in, w_down):
    col_parts = (
        lax.all_gather(w_qkv, "expert", axis=1, tiled=True),
        lax.all_gather(w_out, "expert", axis=1, tiled=True),
        lax.all_gather(w_router, "expert", axis=1, tiled=True),
    )
    return (
        lax.all_gather(col_parts[0], "dp", axis=0, tiled=True),
        lax.all_gather(col_parts[1], "dp", axis=0, tiled=True),
        lax.all_gather(col_parts[2], "dp", axis=0, tiled=True),
        lax.all_gather(w_in, "dp", axis=2, tiled=True),
        lax.all_gather(w_down, "dp", axis=1, tiled=True),
    )


def shards(tokens, w_qkv, w_out, w_router, norm_params, w_in, w_down, routes, threshold, cotangent):
    tok_count = tokens.shape[0]
    images = tok_count // SEQ
    experts = lax.axis_size("expert")
    top_count = routes.shape[1]
    capacity = 15 * top_count * tok_count // (8 * experts)
    full_parts, norm_gains = fetch_forward(w_qkv, w_out, w_router, norm_params, w_in, w_down)
    full_qkv, full_out, full_router, full_in, full_down = full_parts
    gain_rows = norm_gains.astype(jnp.float32)
    source = tokens.astype(jnp.float32)
    first_norm, normed_one, inverse_one = layer_norm(source, gain_rows[0], gain_rows[1])
    first_low = first_norm.astype(jnp.bfloat16)
    qkv_rows = jnp.dot(first_low, full_qkv, preferred_element_type=jnp.float32).astype(jnp.bfloat16)
    qkv_split = qkv_rows.reshape(images, SEQ, 3, HEADS, HEAD)
    queries, key_part, values = (qkv_split[:, :, 0], qkv_split[:, :, 1], qkv_split[:, :, 2])
    scores = scores_of(queries, key_part)
    head_peaks = jnp.max(scores, axis=(0, 2, 3))
    row_peak = jnp.max(scores, axis=-1, keepdims=True)
    log_total = row_peak + jnp.log(jnp.sum(jnp.exp(scores - row_peak), axis=-1, keepdims=True))
    probs_low = jnp.exp(scores - log_total).astype(jnp.bfloat16)
    attn_mixed = jnp.einsum(
        "bhqk,bkhd->bqhd", probs_low, values, preferred_element_type=jnp.float32
    )
    attn_mixed = attn_mixed.reshape(tok_count, D).astype(jnp.bfloat16)
    resid = source + jnp.dot(attn_mixed, full_out, preferred_element_type=jnp.float32)
    peak_logit = lax.pmax(head_peaks, ("dp", "expert"))
    second_norm, normed_two, inverse_two = layer_norm(resid, gain_rows[2], gain_rows[3])
    second_low = second_norm.astype(jnp.bfloat16)
    logits = jnp.dot(second_low, full_router, preferred_element_type=jnp.float32)
    router_probs = jax.nn.softmax(logits, axis=-1)
    expert_ids = jnp.arange(experts, dtype=jnp.int32)
    chosen = (routes[:, :, None] == expert_ids[None, None, :]).astype(jnp.float32)
    gate_weights = jnp.sum(chosen * router_probs[:, None, :], axis=-1)
    flat_routes = routes.reshape(-1)
    onehot = (flat_routes[:, None] == expert_ids[None, :]).astype(jnp.int32)
    before = jnp.cumsum(onehot, axis=0) - onehot
    target_slot = flat_routes * capacity + jnp.sum(before * onehot, axis=1)
    routed = jnp.repeat(second_low, top_count, axis=0)
    outgoing = jnp.zeros((experts * capacity, D), jnp.bfloat16).at[target_slot].set(routed)
    arrived = lax.all_to_all(
        outgoing.reshape(experts, capacity, D), "expert", split_axis=0, concat_axis=0, tiled=True
    )
    arrived = arrived.reshape(experts * capacity, D)
    hidden = jnp.dot(arrived, full_in[0], preferred_element_type=jnp.float32)
    active, gelu_back = jax.vjp(exact_gelu, hidden)
    active_low = active.astype(jnp.bfloat16)
    expert_out = jnp.dot(active_low, full_down[0], preferred_element_type=jnp.float32).astype(
        jnp.bfloat16
    )
    returned = lax.all_to_all(
        expert_out.reshape(experts, capacity, D), "expert", split_axis=0, concat_axis=0, tiled=True
    )
    picked = (
        returned.reshape(experts * capacity, D)[target_slot]
        .astype(jnp.float32)
        .reshape(tok_count, top_count, D)
    )
    output = resid + jnp.sum(picked * gate_weights[:, :, None], axis=1)
    upstream = cotangent.astype(jnp.float32)
    anchor, upstream = lax.optimization_barrier(((w_qkv, w_out, w_router, w_in, w_down), upstream))
    back_qkv, back_out, back_router, back_in, back_down = fetch_backward(
        anchor[0], anchor[1], anchor[2], anchor[3], anchor[4]
    )
    grad_picked = (
        (upstream[:, None, :] * gate_weights[:, :, None])
        .astype(jnp.bfloat16)
        .reshape(tok_count * top_count, D)
    )
    grad_gates = jnp.sum(upstream[:, None, :] * picked, axis=-1)
    grad_probs = jnp.sum(grad_gates[:, :, None] * chosen, axis=1)
    grad_logits = router_probs * (
        grad_probs - jnp.sum(grad_probs * router_probs, axis=-1, keepdims=True)
    )
    back_slots = jnp.zeros((experts * capacity, D), jnp.bfloat16).at[target_slot].set(grad_picked)
    grad_expert = lax.all_to_all(
        back_slots.reshape(experts, capacity, D), "expert", split_axis=0, concat_axis=0, tiled=True
    )
    grad_expert = grad_expert.reshape(experts * capacity, D)
    grad_down = contract_rows(active_low, grad_expert)
    grad_active = contract_cols(grad_expert, back_down[0])
    grad_hidden = gelu_back(grad_active)[0].astype(jnp.bfloat16)
    grad_in = contract_rows(arrived, grad_hidden)
    grad_rows = contract_cols(grad_hidden, back_in[0]).astype(jnp.bfloat16)
    grad_back = lax.all_to_all(
        grad_rows.reshape(experts, capacity, D), "expert", split_axis=0, concat_axis=0, tiled=True
    )
    grad_routed = grad_back.reshape(experts * capacity, D)[target_slot].astype(jnp.float32)
    router_float = back_router.astype(jnp.float32)
    grad_second = jnp.sum(grad_routed.reshape(tok_count, top_count, D), axis=1) + lax.dot_general(
        grad_logits, router_float, (((1,), (1,)), ((), ())), precision=lax.Precision.HIGHEST
    )
    grad_router = lax.dot_general(
        second_low.astype(jnp.float32),
        grad_logits,
        (((0,), (0,)), ((), ())),
        precision=lax.Precision.HIGHEST,
    )
    grad_resid_two, gain_two_grad, shift_two_grad = norm_back(
        grad_second, normed_two, inverse_two, gain_rows[2]
    )
    grad_resid = upstream + grad_resid_two
    grad_resid_low = grad_resid.astype(jnp.bfloat16)
    grad_out = contract_rows(attn_mixed, grad_resid_low)
    grad_mixed = (
        contract_cols(grad_resid_low, back_out)
        .astype(jnp.bfloat16)
        .reshape(images, SEQ, HEADS, HEAD)
    )
    again_scores = scores_of(queries, key_part)
    probs_full = jnp.exp(again_scores - log_total)
    grad_attn = jnp.einsum(
        "bqhd,bkhd->bhqk", grad_mixed, values, preferred_element_type=jnp.float32
    )
    grad_scores = (
        probs_full * (grad_attn - jnp.sum(grad_attn * probs_full, axis=-1, keepdims=True))
    ).astype(jnp.bfloat16)
    grad_queries = jnp.einsum(
        "bhqk,bkhd->bqhd", grad_scores, key_part, preferred_element_type=jnp.float32
    ) * HEAD ** (-0.5)
    grad_keys = jnp.einsum(
        "bhqk,bqhd->bkhd", grad_scores, queries, preferred_element_type=jnp.float32
    ) * HEAD ** (-0.5)
    grad_values = jnp.einsum(
        "bhqk,bqhd->bkhd", probs_low, grad_mixed, preferred_element_type=jnp.float32
    )
    grad_qkv_rows = (
        jnp.stack([grad_queries, grad_keys, grad_values], axis=2)
        .reshape(tok_count, 3 * D)
        .astype(jnp.bfloat16)
    )
    grad_qkv = contract_rows(first_low, grad_qkv_rows)
    grad_first = contract_cols(grad_qkv_rows, back_qkv)
    grad_source, gain_one_grad, shift_one_grad = norm_back(
        grad_first, normed_one, inverse_one, gain_rows[0]
    )
    grad_tokens = (grad_resid + grad_source).astype(jnp.bfloat16)
    norm_grads = jnp.stack([gain_one_grad, shift_one_grad, gain_two_grad, shift_two_grad])
    col_sums = (
        lax.psum_scatter(
            grad_qkv.astype(jnp.bfloat16), "expert", scatter_dimension=1, tiled=True
        ).astype(jnp.float32),
        lax.psum_scatter(
            grad_out.astype(jnp.bfloat16), "expert", scatter_dimension=1, tiled=True
        ).astype(jnp.float32),
        lax.psum_scatter(
            grad_router.astype(jnp.bfloat16), "expert", scatter_dimension=1, tiled=True
        ).astype(jnp.float32),
        lax.psum_scatter(
            norm_grads.astype(jnp.bfloat16), "expert", scatter_dimension=1, tiled=True
        ).astype(jnp.float32),
    )
    row_sums = (
        lax.psum_scatter(
            col_sums[0].astype(jnp.bfloat16), "dp", scatter_dimension=0, tiled=True
        ).astype(jnp.float32),
        lax.psum_scatter(
            col_sums[1].astype(jnp.bfloat16), "dp", scatter_dimension=0, tiled=True
        ).astype(jnp.float32),
        lax.psum_scatter(
            col_sums[2].astype(jnp.bfloat16), "dp", scatter_dimension=0, tiled=True
        ).astype(jnp.float32),
        lax.psum_scatter(
            grad_in[None].astype(jnp.bfloat16), "dp", scatter_dimension=2, tiled=True
        ).astype(jnp.float32),
        lax.psum_scatter(
            grad_down[None].astype(jnp.bfloat16), "dp", scatter_dimension=1, tiled=True
        ).astype(jnp.float32),
    )
    norm_total = lax.psum(col_sums[3], "dp")
    factors = jnp.sqrt(jnp.minimum(1.0, threshold[0].astype(jnp.float32) / peak_logit))
    col_width = w_qkv.shape[1]
    column = lax.axis_index("expert") * col_width + jnp.arange(col_width, dtype=jnp.int32)
    head_index = column % D // HEAD
    head_table = jnp.sum(
        jnp.where(
            head_index[:, None] == jnp.arange(HEADS, dtype=jnp.int32)[None, :],
            factors[None, :],
            0.0,
        ),
        axis=1,
    )
    column_scale = jnp.where(column < 2 * D, head_table, 1.0)
    clipped = (w_qkv.astype(jnp.float32) - LEARN * row_sums[0]) * column_scale[None, :]
    return (
        output.astype(jnp.bfloat16),
        grad_tokens,
        row_sums[0],
        row_sums[1],
        row_sums[2],
        norm_total,
        row_sums[3],
        row_sums[4],
        clipped,
        factors,
    )


def solution(mesh):
    in_specs = (
        P(("dp", "expert"), None),
        P("dp", "expert"),
        P("dp", "expert"),
        P("dp", "expert"),
        P(None, "expert"),
        P("expert", None, "dp"),
        P("expert", "dp", None),
        P(("dp", "expert"), None),
        P(),
        P(("dp", "expert"), None),
    )
    out_specs = (
        P(("dp", "expert"), None),
        P(("dp", "expert"), None),
        P("dp", "expert"),
        P("dp", "expert"),
        P("dp", "expert"),
        P(None, "expert"),
        P("expert", None, "dp"),
        P("expert", "dp", None),
        P("dp", "expert"),
        P(),
    )
    return jax.shard_map(shards, mesh=mesh, in_specs=in_specs, out_specs=out_specs, check_vma=False)
```

profile of v0, /device:TPU:0, one launch (start us, length us, event | category | flops | bytes accessed | tf_op | source)
XLA Modules:
  0.0 813.2 jit_solution(14412954212243499259)
XLA Ops:
  7.3 35.2 %all_gather.52 = bf16[128,1536]{0,1:T(8,128)(2,1)} all-gather(bf16[128,192]{0,1:T(8,128)(2,1)} %param.11), channel_id=1, replica_groups=mesh['dp'=4,'expert'=8] {'expert'}, dimensions={1}, use_global_device_ids=true | all-gather | bytes 442368 | tf_op jit(solution)/shard_map/all_gather | solution.py:58
  46.0 30.5 %all_gather.54 = bf16[128,512]{0,1:T(8,128)(2,1)S(1)} all-gather(bf16[128,64]{0,1:T(8,128)(2,1)S(1)} %copy-done.17), channel_id=1, replica_groups=mesh['dp'=4,'expert'=8] {'expert'}, dimensions={1}, use_global_device_ids=true | all-gather | bytes 147456 | tf_op jit(solution)/shard_map/all_gather | solution.py:59
  77.2 20.5 %all-gather = bf16[8,64,4]{1,2,0:T(4,128)(2,1)S(1)} all-gather(bf16[1,64,4]{1,2,0:T(4,128)(2,1)S(1)} %bitcast.149), channel_id=1, replica_groups=mesh['dp'=4,'expert'=8] {'expert'}, dimensions={0}, use_global_device_ids=true | all-gather | bytes 4608 | tf_op jit(solution)/shard_map/all_gather | solution.py:61
  97.8 10.8 %all_gather.55 = bf16[512,512]{0,1:T(8,128)(2,1)} all-gather(bf16[128,512]{0,1:T(8,128)(2,1)S(1)} %all_gather.54), channel_id=1, replica_groups=mesh['dp'=4,'expert'=8] {'dp'}, dimensions={0}, use_global_device_ids=true | all-gather | bytes 655360 | tf_op jit(solution)/shard_map/all_gather | solution.py:65
  141.8 7.5 scatter_custom_fusion
  154.2 40.3 %all-gather.1 = bf16[8,1,128]{2,1,0:T(2,128)(2,1)S(1)} all-gather(bf16[1,1,128]{2,1,0:T(2,128)(2,1)S(1)} %bitcast.146), channel_id=1, replica_groups=mesh['dp'=4,'expert'=8] {'expert'}, dimensions={0}, use_global_device_ids=true | all-gather | bytes 2304 | tf_op jit(solution)/shard_map/all_gather | solution.py:60
  208.5 10.0 %scatter_custom_fusion.1 = bf16[1472,512]{1,0:T(8,128)(2,1)} fusion(s32[788]{0:T(1024)S(1)} %fusion.56, f32[788,512]{1,0:T(8,128)} %mul.265, f32[788]{0:T(1024)S(1)} %mul.266, bf16[]{:T(256)} %constant.55.clone.1), kind=kCustom, calls=%fused_computation.83 | custom fusion | flops 806912 | bytes 3125250 | tf_op jit(solution)/shard_map/scatter | solution.py:161
  218.6 7.4 all-to-all-start.2
  226.0 31.0 %multiply_convert_fusion = (bf16[1472,2048]{1,0:T(8,128)(2,1)}, f32[1472,2048]{1,0:T(8,128)}, f32[1472,2048]{1,0:T(8,128)}) fusion(bf16[1472,512]{1,0:T(8,128)(2,1)} %bitcast.16, bf16[1,512,2048]{2,1,0:T(8,128)(2,1)} %all-gather.12.cloned.1.call-done), kind=kOutput, calls=%fused_computation.7 | convolution fusion | flops 3282960384 | bytes 33751040 | tf_op jit(solution)/shard_map/dot_general | solution.py:131
  256.9 7.8 convolution_convert_fusion.4
  264.7 6.5 all-to-all-start.1
  271.3 15.1 %add_convert_fusion = bf16[1472,2048]{1,0:T(8,128)(2,1)} fusion(f32[1472,2048]{1,0:T(8,128)} %get-tuple-element.37, f32[1472,2048]{1,0:T(8,128)} %get-tuple-element.51, bf16[1472,512]{1,0:T(8,128)(2,1)} %bitcast.24, bf16[1,2048,512]{2,1,0:T(8,128)(2,1)} %all-gather.16.cloned.1.call-done), kind=kOutput, calls=%fused_computation.6 | convolution fusion | flops 3129212928 | bytes 33751040 | tf_op jit(solution)/shard_map/dot_general | solution.py:51
  286.4 7.9 convolution_convert_fusion.3
  294.3 12.5 %all-to-all-done.1 = bf16[8,184,512]{2,1,0:T(8,128)(2,1)} async-done(((bf16[8,184,512]{2,1,0:T(8,128)(2,1)}), bf16[8,184,512]{2,1,0:T(8,128)(2,1)}, u32[]{:S(2)}, u32[]{:S(2)}) %all-to-all-start.1) | async-done | bytes 1507360 | tf_op jit(solution)/shard_map/all_to_all | solution.py:137
  311.2 57.9 %all_gather.66 = bf16[128,1536]{0,1:T(8,128)(2,1)} all-gather(bf16[128,192]{0,1:T(8,128)(2,1)S(1)} %copy-done.12), channel_id=1, replica_groups=mesh['dp'=4,'expert'=8] {'expert'}, dimensions={1}, use_global_device_ids=true | all-gather | bytes 442368 | tf_op jit(solution)/shard_map/all_gather | solution.py:75
  369.1 18.7 %all-gather.2 = bf16[8,1,128]{2,1,0:T(2,128)(2,1)S(1)} all-gather(bf16[1,1,128]{2,1,0:T(2,128)(2,1)} %bitcast.145), channel_id=1, replica_groups=mesh['dp'=4,'expert'=8] {'expert'}, dimensions={0}, use_global_device_ids=true | all-gather | bytes 2304 | tf_op jit(solution)/shard_map/all_gather | solution.py:77
  393.4 30.7 %all_gather.64 = bf16[128,512]{0,1:T(8,128)(2,1)S(1)} all-gather(bf16[128,64]{0,1:T(8,128)(2,1)} %param.12), channel_id=1, replica_groups=mesh['dp'=4,'expert'=8] {'expert'}, dimensions={1}, use_global_device_ids=true | all-gather | bytes 147456 | tf_op jit(solution)/shard_map/all_gather | solution.py:76
  425.4 7.5 all_gather.65
  441.6 6.3 multiply_reduce_fusion.3
  498.0 17.6 %all-reduce.1 = bf16[512,8]{0,1:T(8,128)(2,1)S(1)} all-reduce(bf16[512,8]{0,1:T(8,128)(2,1)S(1)} %convolution_convert_fusion.10), channel_id=6, replica_groups=mesh['dp'=4,'expert'=8] {'expert'}, use_global_device_ids=true, to_apply=%region_28.29.clone | all-reduce | flops 4096 | bytes 16384
  518.0 21.6 %reduce-scatter.19.cloned.1.call-done = bf16[512,64]{0,1:T(8,128)(2,1)} async-done(((bf16[512,512]{0,1:T(8,128)(2,1)}), bf16[512,64]{0,1:T(8,128)(2,1)}) %reduce-scatter.19.cloned.1.call-update) | async-done | bytes 65552 | tf_op jit(solution)/shard_map/reduce_scatter | solution.py:229
  541.6 8.0 fusion.7
  549.6 8.0 fusion.6
  558.4 40.2 %pmax.7 = f32[8]{0:T(128)S(1)} all-reduce(f32[8]{0:T(128)S(1)} %get-tuple-element.22), channel_id=1, replica_groups=mesh['dp'=4,'expert'=8] {'dp','expert'}, use_global_device_ids=true, to_apply=%region_39.40 | all-reduce | flops 8 | bytes 64 | tf_op jit(solution)/shard_map/pmax | solution.py:113
  598.7 8.7 %reduce-scatter.17.cloned.1.call-done = bf16[512,192]{0,1:T(8,128)(2,1)} async-done(((bf16[512,1536]{0,1:T(8,128)(2,1)}), bf16[512,192]{0,1:T(8,128)(2,1)}) %reduce-scatter.17.cloned.1.call-update) | async-done | bytes 196624 | tf_op jit(solution)/shard_map/reduce_scatter | solution.py:226
  610.3 18.1 %reduce-scatter.29.cloned.1.call-done = bf16[128,1]{1,0:T(8,128)(2,1)} async-done(((bf16[512,1]{1,0:T(8,128)(2,1)}), bf16[128,1]{1,0:T(8,128)(2,1)}) %reduce-scatter.29.cloned.1.call-update) | async-done | bytes 272
  629.8 63.0 %reduce-scatter.31.cloned.1.call-done = bf16[64,4]{1,0:T(8,128)(2,1)} async-done(((bf16[512,4]{1,0:T(8,128)(2,1)}), bf16[64,4]{1,0:T(8,128)(2,1)}) %reduce-scatter.31.cloned.1.call-update) | async-done | bytes 528
  693.6 6.2 psum.7
  699.8 14.2 %reduce-scatter.27.cloned.1.call-done = bf16[128,64]{1,0:T(8,128)(2,1)} async-done(((bf16[512,64]{1,0:T(8,128)(2,1)}), bf16[128,64]{1,0:T(8,128)(2,1)}) %reduce-scatter.27.cloned.1.call-update) | async-done | bytes 16400
  715.5 32.4 %reduce-scatter.23.cloned.1.call-done = bf16[1,512,512]{2,1,0:T(8,128)(2,1)} async-done(((bf16[1,2048,512]{2,1,0:T(8,128)(2,1)}), bf16[1,512,512]{2,1,0:T(8,128)(2,1)}) %reduce-scatter.23.cloned.1.call-update) | async-done | bytes 524304 | tf_op jit(solution)/shard_map/reduce_scatter | solution.py:252
  750.1 32.0 %reduce-scatter.21.cloned.1.call-done = bf16[1,512,512]{2,1,0:T(8,128)(2,1)} async-done(((bf16[1,512,2048]{2,1,0:T(8,128)(2,1)}), bf16[1,512,512]{2,1,0:T(8,128)(2,1)}) %reduce-scatter.21.cloned.1.call-update) | async-done | bytes 524304 | tf_op jit(solution)/shard_map/reduce_scatter | solution.py:249
  784.2 20.3 %reduce-scatter.25.cloned.1.call-done = bf16[128,192]{1,0:T(8,128)(2,1)} async-done(((bf16[512,192]{1,0:T(8,128)(2,1)}), bf16[128,192]{1,0:T(8,128)(2,1)}) %reduce-scatter.25.cloned.1.call-update) | async-done | bytes 49168
  (229 shorter events, 142.9 us)
Async XLA Ops:
  7.2 38.8 %copy-start.17 = (bf16[128,64]{0,1:T(8,128)(2,1)S(1)}, bf16[128,64]{0,1:T(8,128)(2,1)}, u32[]{:S(2)}) copy-start(bf16[128,64]{0,1:T(8,128)(2,1)} %param.12) | copy-start | bytes 49156
  7.2 69.4 %copy-start.18 = (s32[394,2]{0,1:T(2,128)S(1)}, s32[394,2]{0,1:T(2,128)}, u32[]{:S(2)}) copy-start(s32[394,2]{0,1:T(2,128)} %param.17) | copy-start | bytes 9460
  7.2 69.5 %copy-start.6 = (bf16[394,512]{1,0:T(8,128)(2,1)S(1)}, bf16[394,512]{1,0:T(8,128)(2,1)}, u32[]{:S(2)}) copy-start(bf16[394,512]{1,0:T(8,128)(2,1)} %param.10) | copy-start | bytes 1210372
  7.2 70.0 %copy-start.38 = (bf16[4,64]{1,0:T(4,128)(2,1)S(1)}, bf16[4,64]{1,0:T(4,128)(2,1)}, u32[]{:S(2)}) copy-start(bf16[4,64]{1,0:T(4,128)(2,1)} %param.14) | copy-start | bytes 1540
  7.2 104.5 %all-gather.10.cloned.1.call-start = ((), (), s32[]{:S(2)}) async-start(), calls=%async_computation.12 | async-start | bytes 1966080 | tf_op jit(solution)/shard_map/all_gather | solution.py:64
  42.5 183.5 %all-gather.12.cloned.1.call-start = ((), (), s32[]{:S(2)}) async-start(), calls=%async_computation.13 | async-start | bytes 2621440 | tf_op jit(solution)/shard_map/all_gather | solution.py:67
  43.2 213.7 %all-gather.14.cloned.1.call-start = ((), (), s32[]{:S(2)}) async-start(), calls=%async_computation.14 | async-start | bytes 2621440 | tf_op jit(solution)/shard_map/all_gather | solution.py:68
  44.0 227.3 %all-gather.16.cloned.1.call-start = ((), (), s32[]{:S(2)}) async-start(), calls=%async_computation.15 | async-start | bytes 2621440 | tf_op jit(solution)/shard_map/all_gather | solution.py:84
  76.9 41.3 %copy-start.28 = (f32[394]{0:T(512)}, f32[394]{0:T(512)S(1)}, u32[]{:S(2)}) copy-start(f32[394]{0:T(512)S(1)} %broadcast_multiply_fusion.6) | copy-start | bytes 4732
  77.2 41.0 %copy-start.31 = (f32[394]{0:T(512)}, f32[394]{0:T(512)S(1)}, u32[]{:S(2)}) copy-start(f32[394]{0:T(512)S(1)} %add_rsqrt_fusion.1) | copy-start | bytes 4732
  97.8 14.0 %copy-start.36 = (f32[1,512]{1,0:T(1,128)}, f32[1,512]{1,0:T(1,128)S(1)}, u32[]{:S(2)}) copy-start(f32[1,512]{1,0:T(1,128)S(1)} %get-tuple-element.45) | copy-start | bytes 6148
  97.8 38.1 %copy-start.24 = (f32[1,512]{1,0:T(1,128)}, f32[1,512]{1,0:T(1,128)S(1)}, u32[]{:S(2)}) copy-start(f32[1,512]{1,0:T(1,128)S(1)} %get-tuple-element.43) | copy-start | bytes 6148
  111.7 96.8 %copy-start.30 = (s32[788]{0:T(1024)}, s32[788]{0:T(1024)S(1)}, u32[]{:S(2)}) copy-start(s32[788]{0:T(1024)S(1)} %fusion.56) | copy-start | bytes 9460
  138.8 15.4 %copy-start.35 = (bf16[128,1]{0,1:T(2,128)(2,1)S(1)}, bf16[128,1]{0,1:T(2,128)(2,1)}, u32[]{:S(2)}) copy-start(bf16[128,1]{0,1:T(2,128)(2,1)} %param.13) | copy-start | bytes 772
  149.3 69.3 %all-to-all-start = ((bf16[8,184,512]{2,1,0:T(8,128)(2,1)}), bf16[8,184,512]{2,1,0:T(8,128)(2,1)}, u32[]{:S(2)}, u32[]{:S(2)}) async-start(bf16[8,184,512]{2,1,0:T(8,128)(2,1)} %bitcast.126), calls=%async_computation | async-start | bytes 3014656 | tf_op jit(solution)/shard_map/all_to_all | solution.py:127
  153.6 132.8 %all-gather.18.cloned.1.call-start = ((), (), s32[]{:S(2)}) async-start(), calls=%async_computation.16 | async-start | bytes 2621440 | tf_op jit(solution)/shard_map/all_gather | solution.py:83
  218.6 46.2 %all-to-all-start.2 = ((bf16[8,184,512]{2,1,0:T(8,128)(2,1)}), bf16[8,184,512]{2,1,0:T(8,128)(2,1)}, u32[]{:S(2)}, u32[]{:S(2)}) async-start(bf16[8,184,512]{2,1,0:T(8,128)(2,1)} %bitcast.127), calls=%async_computation.2 | async-start | bytes 3014656 | tf_op jit(solution)/shard_map/all_to_all | solution.py:162
  264.7 42.1 %all-to-all-start.1 = ((bf16[8,184,512]{2,1,0:T(8,128)(2,1)}), bf16[8,184,512]{2,1,0:T(8,128)(2,1)}, u32[]{:S(2)}, u32[]{:S(2)}) async-start(bf16[8,184,512]{2,1,0:T(8,128)(2,1)} %bitcast.129), calls=%async_computation.1 | async-start | bytes 3014656 | tf_op jit(solution)/shard_map/all_to_all | solution.py:137
  286.4 24.7 %copy-start.12 = (bf16[128,192]{0,1:T(8,128)(2,1)S(1)}, bf16[128,192]{0,1:T(8,128)(2,1)}, u32[]{:S(2)}) copy-start(bf16[128,192]{0,1:T(8,128)(2,1)} %param.11) | copy-start | bytes 147460
  306.8 142.2 %all-to-all-start.3 = ((bf16[8,184,512]{2,1,0:T(8,128)(2,1)}), bf16[8,184,512]{2,1,0:T(8,128)(2,1)}, u32[]{:S(2)}, u32[]{:S(2)}) async-start(bf16[8,184,512]{2,1,0:T(8,128)(2,1)} %bitcast.128), calls=%async_computation.3 | async-start | bytes 3014656 | tf_op jit(solution)/shard_map/all_to_all | solution.py:171
  311.1 183.4 %all-gather.20.cloned.1.call-start = ((), (), s32[]{:S(2)}) async-start(), calls=%async_computation.17 | async-start | bytes 1966080 | tf_op jit(solution)/shard_map/all_gather | solution.py:80
  369.1 170.6 %reduce-scatter.19.cloned.1.call-start = ((), (), s32[]{:S(2)}) async-start(), calls=%async_computation.19 | async-start | bytes 589824 | tf_op jit(solution)/shard_map/reduce_scatter | solution.py:229
  480.9 126.5 %reduce-scatter.17.cloned.1.call-start = ((), (), s32[]{:S(2)}) async-start(), calls=%async_computation.18 | async-start | bytes 1769472 | tf_op jit(solution)/shard_map/reduce_scatter | solution.py:226
  493.8 134.6 %reduce-scatter.29.cloned.1.call-start = ((), (), s32[]{:S(2)}) async-start(), calls=%async_computation.24 | async-start | bytes 163840
  517.1 175.8 %reduce-scatter.31.cloned.1.call-start = ((), (), s32[]{:S(2)}) async-start(), calls=%async_computation.25 | async-start | bytes 147456
  518.0 196.1 %reduce-scatter.27.cloned.1.call-start = ((), (), s32[]{:S(2)}) async-start(), calls=%async_computation.23 | async-start | bytes 163840
  541.3 206.6 %reduce-scatter.23.cloned.1.call-start = ((), (), s32[]{:S(2)}) async-start(), calls=%async_computation.21 | async-start | bytes 2621440 | tf_op jit(solution)/shard_map/reduce_scatter | solution.py:252
  549.6 232.5 %reduce-scatter.21.cloned.1.call-start = ((), (), s32[]{:S(2)}) async-start(), calls=%async_computation.20 | async-start | bytes 2621440 | tf_op jit(solution)/shard_map/reduce_scatter | solution.py:249
  557.6 51.7 %copy-start.3 = (f32[394,512]{1,0:T(8,128)S(1)}, f32[394,512]{1,0:T(8,128)}, u32[]{:S(2)}) copy-start(f32[394,512]{1,0:T(8,128)} %copy-done.2) | copy-start | bytes 2420740
  557.6 51.7 %copy-start.11 = (f32[394,512]{1,0:T(8,128)S(1)}, f32[394,512]{1,0:T(8,128)}, u32[]{:S(2)}) copy-start(f32[394,512]{1,0:T(8,128)} %get-tuple-element.56) | copy-start | bytes 2420740
  557.6 246.9 %reduce-scatter.25.cloned.1.call-start = ((), (), s32[]{:S(2)}) async-start(), calls=%async_computation.22 | async-start | bytes 327680
  598.6 206.9 %copy-start.39 = (f32[8]{0:T(128)}, f32[8]{0:T(128)S(1)}, u32[]{:S(2)}) copy-start(f32[8]{0:T(128)S(1)} %minimum_sqrt_fusion) | copy-start | bytes 100
  (27 other events, 127.5 us)
Sparse Core Ops, SparseCore 0:
  42.6 20.7 all-gather.9
  65.0 22.5 all-gather.11
  89.1 25.3 all-gather.13
  116.0 20.6 all-gather.15
  155.7 23.5 all-gather.17
  369.2 18.6 all-gather.19
  481.0 58.5 reduce-scatter.18
  543.5 63.9 reduce-scatter.16
  609.9 18.5 reduce-scatter.28
  632.0 60.8 reduce-scatter.30
  695.4 18.6 reduce-scatter.26
  716.4 31.4 reduce-scatter.22
  750.6 31.4 reduce-scatter.20
  784.4 20.0 reduce-scatter.24
where the time goes:
time: 825 us; the launch traced here: 813 us
  blocking collectives  327 us (40%)
  waiting for transfers between devices  225 us (27%)
  matrix products  108 us (13%)
  local copies, waits for them, and re-layouts  73.7 us (9%)
  other arithmetic  40.2 us (5%)
  starting transfers between devices  23.3 us (3%)
  between operations  16 us (2%)
    unnamed x18, waiting for transfers between devices  118 us
    all_gather x1, blocking collectives, fetch_backward(): lax.all_gather(w_qkv, 'expert', axis=1, tiled=True)  57.9 us
    all_gather x1, blocking collectives, fetch_forward(): lax.all_gather(w_router, 'expert', axis=1, tiled=True)  40.3 us
    pmax x1, blocking collectives, shards(): peak_logit = lax.pmax(head_peaks, ('dp', 'expert'))  40.2 us
    all_gather x1, blocking collectives, fetch_forward(): lax.all_gather(w_qkv, 'expert', axis=1, tiled=True)  35.2 us
    reduce_scatter x1, waiting for transfers between devices, shards(): lax.psum_scatter(grad_down[None].astype(jnp.bfloat16), 'dp', scatter_dime...  32.4 us
    reduce_scatter x1, waiting for transfers between devices, shards(): lax.psum_scatter(grad_in[None].astype(jnp.bfloat16), 'dp', scatter_dimens...  32 us
    dot_general x1, matrix products, shards(): hidden = jnp.dot(arrived, full_in[0], preferred_element_type=jnp.float32)  31 us
  transfers between devices with their start and end apart: 18, of which 9 were waited for; matrix products, arithmetic and copies ran while one was open for 27% of the time, Pallas kernels for 0%

commit v1 on v0

--- a/solution.py
+++ b/solution.py
@@ -1,16 +1,595 @@
+import functools
+
 import jax
 import jax.numpy as jnp
 from jax import lax
+from jax.experimental import pallas as pl
+from jax.experimental.pallas import tpu as pltpu
 from jax.sharding import PartitionSpec as P
 
 D = 512
 HEADS = 8
 HEAD = 64
 SEQ = 197
-
-
 EPS = 1e-06
 LEARN = 0.001
+SEQP = 208
+BF = jnp.bfloat16
+F32 = jnp.float32
+MESH = pl.DeviceIdType.MESH
+
+(DENSE_E, DENSE_Y, DENSE_C, EXPW, COT, ACT, GATE, DXE, ZED, DGATE, WGC, WGY, RSC, RSY, RSE, SMC, SME) = range(17)
+
+
+def dg(left, right, left_dim, right_dim):
+    return lax.dot_general(
+        left, right, (((left_dim,), (right_dim,)), ((), ())), preferred_element_type=F32
+    )
+
+
+def iota(shape, dim):
+    return lax.broadcasted_iota(jnp.int32, shape, dim)
+
+
+def eye(size, dtype=BF):
+    return (iota((size, size), 0) == iota((size, size), 1)).astype(F32).astype(dtype)
+
+
+def split_two(value):
+    high = value.astype(BF)
+    return high, (value - high.astype(F32)).astype(BF)
+
+
+def to_row(column):
+    size = column.shape[0]
+    return jnp.sum(jnp.where(iota((size, size), 0) == iota((size, size), 1), column, 0.0), axis=0, keepdims=True)
+
+
+def to_column(row):
+    size = row.shape[1]
+    return jnp.sum(jnp.where(iota((size, size), 0) == iota((size, size), 1), row, 0.0), axis=1, keepdims=True)
+
+
+def norm_parts(values):
+    centered = values - jnp.mean(values, axis=-1, keepdims=True)
+    inverse = lax.rsqrt(jnp.mean(centered * centered, axis=-1, keepdims=True) + EPS)
+    return centered * inverse, inverse
+
+
+def norm_back(upstream, normed, inverse, gain):
+    scaled = upstream * gain
+    inner = scaled - jnp.mean(scaled, axis=-1, keepdims=True)
+    inner = inner - normed * jnp.mean(scaled * normed, axis=-1, keepdims=True)
+    return (
+        inverse * inner,
+        jnp.sum(upstream * normed, axis=0, keepdims=True),
+        jnp.sum(upstream, axis=0, keepdims=True),
+    )
+
+
+def normal_parts(u):
+    size = jnp.abs(u)
+    t = 1.0 / (1.0 + (0.3275911 * 2.0 ** -0.5) * size)
+    poly = t * (0.254829592 + t * (-0.284496736 + t * (1.421413741 + t * (-1.453152027 + t * 1.061405429))))
+    bell = jnp.exp(-0.5 * u * u)
+    tail = 0.5 * poly * bell
+    return jnp.where(u >= 0, 1.0 - tail, tail), u * (bell * 0.3989422804014327)
+
+
+def block_kernel(
+    n_e, cap, rows,
+    tok, cot, routes, w_qkv, w_out, w_router, norm, win, wdown, threshold,
+    block_out, grad_tok, grad_qkv, grad_out, grad_router, grad_norm, grad_in, grad_down, clipped, factors,
+    GB, WI, WD, XF, CP, R, A1, A2, QKV, O, PS, SEL, SELT, SLOT, NRM, PR, WR,
+    SA, SB, CR, AR, ZR, DXR, GS, GR, GCOL, DGS, DGR, H, DU, DZ,
+    WCS, WCR, WYS, WYR, DQKV, DO, DR, GG, RCR, RYS, RYR, RES, RER, SM, SMCR, SMER,
+    send, recv, local,
+):
+    dp = lax.axis_index("dp")
+    me = lax.axis_index("expert")
+    core = lax.rem(dp, 2)
+    dp_c = dp + 1 - 2 * core
+    dp_y = lax.rem(dp + 2, 4)
+    dp_cy = lax.rem(dp_c + 2, 4)
+    images = rows // SEQ
+    T = images * SEQP
+    part = 3 * D // n_e
+    opart = D // n_e
+    bundle = part + opart + 16
+
+    def at_off(i):
+        return lax.rem(me + i, n_e)
+
+    def from_off(i):
+        return lax.rem(me + n_e - i, n_e)
+
+    def remote(src, dst, kind, i, where):
+        return pltpu.make_async_remote_copy(
+            src_ref=src, dst_ref=dst, send_sem=send.at[kind, i], recv_sem=recv.at[kind, i],
+            device_id=where, device_id_type=MESH,
+        )
+
+    def brow(e, start=0, size=None):
+        return pl.ds(pl.multiple_of(bundle * e + start, 16), bundle if size is None else size)
+
+    peers = [(dp, at_off(i)) for i in range(1, n_e)] + [(dp_y, me), (dp_c, me)]
+    barrier = pltpu.get_barrier_semaphore()
+    for p in peers:
+        pl.semaphore_signal(barrier, inc=1, device_id=p, device_id_type=MESH)
+    load_in = pltpu.make_async_copy(win, WI.at[dp], local.at[0])
+    load_down = pltpu.make_async_copy(wdown, WD.at[dp], local.at[1])
+    load_in.start()
+    load_down.start()
+
+    GB[dp, brow(me, 0, part), :] = dg(eye(part), w_qkv[...], 1, 1).astype(BF)
+    GB[dp, brow(me, part, opart), :] = dg(eye(opart), w_out[...], 1, 1).astype(BF)
+    spread = (iota((16, 4), 0) == iota((16, 4), 1)).astype(F32).astype(BF)
+    twice = (lax.rem(iota((HEAD, 128), 1), HEAD) == iota((HEAD, 128), 0)).astype(F32).astype(BF)
+    small = dg(dg(spread, norm[...], 1, 0).astype(BF), twice, 1, 0)
+    router_row = to_row(w_router[...].astype(F32))
+    small = jnp.where(iota((16, 128), 0) == 8, router_row, small)
+    GB[dp, brow(me, part + opart, 16), :] = small.astype(BF)
+
+    pl.semaphore_wait(barrier, len(peers))
+
+    def dense_e(i, e, where):
+        return remote(GB.at[dp, brow(e)], GB.at[dp, brow(e)], DENSE_E, i, where)
+
+    def dense_y(i):
+        e = from_off(i)
+        return remote(GB.at[dp, brow(e)], GB.at[dp, brow(e)], DENSE_Y, i, (dp_y, me))
+
+    def dense_c(i):
+        d = dp if i == 0 else dp_y
+        return remote(GB.at[d], GB.at[d], DENSE_C, i, (dp_c, me))
+
+    for i in range(1, n_e):
+        dense_e(i, me, (dp, at_off(i))).start()
+    dense_y(0).start()
+
+    move = ((lax.div(iota((T, rows), 0), SEQP) * SEQ + lax.rem(iota((T, rows), 0), SEQP) == iota((T, rows), 1))
+            & (lax.rem(iota((T, rows), 0), SEQP) < SEQ)).astype(F32).astype(BF)
+    CP[...] = dg(move, cot[...], 1, 0).astype(BF)
+    XF[...] = dg(move, tok[...], 1, 0)
+    away = routes[...] - me
+    away = jnp.where(away < 0, away + n_e, away)
+    named = (away[:, 0:1] == iota((rows, n_e), 1)) | (away[:, 1:2] == iota((rows, n_e), 1))
+    chosen = dg(move, named.astype(F32).astype(BF), 1, 0)
+    before = (iota((T, T), 1) < iota((T, T), 0)).astype(F32).astype(BF)
+    chosen_low = chosen.astype(BF)
+    slot = jnp.where(chosen > 0.5, dg(before, chosen_low, 1, 0), -1.0)
+    SLOT[...] = slot
+    chosen_t = dg(eye(n_e), chosen_low, 1, 1)
+    slot_t = jnp.where(chosen_t > 0.5, dg(chosen_t.astype(BF), before, 1, 1), -1.0)
+    lane = iota((T, 2 * cap), 1).astype(F32)
+    for k in range(n_e // 2):
+        target = jnp.where(lane < cap, slot[:, 2 * k:2 * k + 1], slot[:, 2 * k + 1:2 * k + 2] + cap)
+        SELT[:, 2 * cap * k:2 * cap * (k + 1)] = (lane == target).astype(F32).astype(BF)
+    level = iota((cap, T), 0).astype(F32)
+    for i in range(n_e):
+        SEL[i] = (level == slot_t[i:i + 1, :]).astype(F32).astype(BF)
+        packed = dg(SEL[i], CP[...], 1, 0).astype(BF)
+        if i == 0:
+            CR[0:cap] = packed
+        else:
+            SA[cap * i:cap * (i + 1)] = packed
+
+    for i in range(1, n_e):
+        dense_e(i, from_off(i), (dp, at_off(i))).wait_recv()
+        dense_y(i).start()
+    dense_c(0).start()
+
+    load_in.wait()
+    load_down.wait()
+
+    def exp_w(k):
+        buf = WI if k % 2 == 0 else WD
+        if k < 2:
+            return remote(buf.at[dp], buf.at[dp], EXPW, k, (dp_y, me))
+        d = dp if k < 4 else dp_y
+        return remote(buf.at[d], buf.at[d], EXPW, k, (dp_c, me))
+
+    for k in range(4):
+        exp_w(k).start()
+
+    def to_expert(buf_s, buf_r, kind, i):
+        return remote(buf_s.at[pl.ds(cap * i, cap)], buf_r.at[pl.ds(cap * i, cap)], kind, i, (dp, at_off(i)))
+
+    def to_token(buf_s, buf_r, kind, i):
+        return remote(buf_s.at[pl.ds(cap * i, cap)], buf_r.at[pl.ds(cap * i, cap)], kind, i, (dp, from_off(i)))
+
+    for i in range(1, n_e):
+        to_expert(SA, CR, COT, i).start()
+
+    half = iota((16, 128), 1) < HEAD
+    pieces = []
+    for k in range(D // 128):
+        even = GB[dp, brow(2 * k, part + opart, 16), :].astype(F32)
+        odd = GB[dp, brow(2 * k + 1, part + opart, 16), :].astype(F32)
+        pieces.append(jnp.where(half, even, odd))
+    NRM[...] = jnp.concatenate(pieces, axis=1)
+    normed, _ = norm_parts(XF[...])
+    A1[...] = (normed * NRM[0:1] + NRM[1:2]).astype(BF)
+
+    for i in range(n_e):
+        dense_y(i).wait_recv()
+    dense_c(1).start()
+    dense_c(0).wait_recv()
+    dense_c(1).wait_recv()
+
+    def dense_rows(e, start, size):
+        return jnp.concatenate([GB[d, brow(e, start, size), :] for d in range(4)], axis=1)
+
+    def qkv_weight(k):
+        return jnp.concatenate([dense_rows(2 * k, 0, part), dense_rows(2 * k + 1, 0, part)], axis=0)
+
+    def out_weight():
+        return jnp.concatenate([dense_rows(e, part, opart) for e in range(n_e)], axis=0)
+
+    for k in range(n_e // 2):
+        QKV[:, 2 * part * k:2 * part * (k + 1)] = dg(A1[...], qkv_weight(k), 1, 1).astype(BF)
+
+    row_ok = iota((SEQP, SEQP), 0) < SEQ
+    col_ok = iota((SEQP, SEQP), 1) < SEQ
+    first_head = iota((1, 128), 1) < HEAD
+    masks = [first_head.astype(F32).astype(BF), (~first_head).astype(F32).astype(BF)]
+
+    def attend(g, peaks):
+        img = lax.div(g, HEADS // 2)
+        pair = lax.rem(g, HEADS // 2)
+        at = pl.ds(pl.multiple_of(SEQP * img, 16), SEQP)
+        q2 = QKV[at, pl.ds(pl.multiple_of(128 * pair, 128), 128)]
+        k2 = QKV[at, pl.ds(pl.multiple_of(D + 128 * pair, 128), 128)]
+        v2 = QKV[at, pl.ds(pl.multiple_of(2 * D + 128 * pair, 128), 128)]
+        mixed = jnp.zeros((SEQP, 128), F32)
+        for hh in range(2):
+            s = dg(q2 * masks[hh], k2, 1, 1) * HEAD ** -0.5
+            s = jnp.where(col_ok, s, -1e30)
+            top = jnp.max(s, axis=1, keepdims=True)
+            ex = jnp.exp(s - top)
+            p = ex / jnp.sum(ex, axis=1, keepdims=True)
+            PS[2 * g + hh] = p
+            mixed = mixed + dg(p.astype(BF), v2 * masks[hh], 1, 0)
+            peak = jnp.max(jnp.where(row_ok, s, -1e30), axis=(0, 1), keepdims=True)
+            peaks = jnp.where(iota((8, 128), 0) == 2 * pair + hh, jnp.maximum(peaks, peak), peaks)
+        O[at, pl.ds(pl.multiple_of(128 * pair, 128), 128)] = mixed.astype(BF)
+        return peaks
+
+    peaks = lax.fori_loop(0, images * HEADS // 2, attend, jnp.full((8, 128), -1e30, F32))
+    for k in range(D // 128):
+        SM[0, k, 8:16, :] = peaks
+
+    for k in range(2):
+        exp_w(k).wait_recv()
+        exp_w(4 + k).start()
+
+    R[...] = XF[...] + dg(O[...], out_weight(), 1, 1)
+    normed, _ = norm_parts(R[...])
+    A2[...] = (normed * NRM[2:3] + NRM[3:4]).astype(BF)
+    router = jnp.zeros((n_e, D), F32)
+    for i in range(n_e):
+        at = dense_rows(at_off(i), part + opart, 16).astype(F32)
+        router = jnp.where(iota((n_e, D), 0) == i, at[8:9, :], router)
+    WR[...] = router.astype(BF)
+    logits = dg(A2[...], WR[...], 1, 1)
+    ex = jnp.exp(logits - jnp.max(logits, axis=1, keepdims=True))
+    PR[...] = ex / jnp.sum(ex, axis=1, keepdims=True)
+    lane_cap = iota((T, cap), 1).astype(F32)
+    for i in range(n_e):
+        packed = dg(SEL[i], A2[...], 1, 0).astype(BF)
+        gate = jnp.sum(jnp.where(lane_cap == SLOT[:, i:i + 1], PR[:, i:i + 1], 0.0), axis=0, keepdims=True)
+        if i == 0:
+            AR[0:cap] = packed
+            GR[0] = jnp.broadcast_to(gate, (8, cap))
+        else:
+            SB[cap * i:cap * (i + 1)] = packed
+            GS[i] = jnp.broadcast_to(gate, (8, cap))
+            remote(GS.at[i], GR.at[i], GATE, i, (dp, at_off(i))).start()
+            to_expert(SB, AR, ACT, i).start()
+
+    for k in range(2, 6):
+        exp_w(k).wait_recv()
+
+    pairs = n_e // 2
+    for j in range(pairs):
+        mine = pl.ds(2 * cap * j, 2 * cap)
+        gates = []
+        for i in (2 * j, 2 * j + 1):
+            if i > 0:
+                to_expert(SA, CR, COT, i).wait_recv()
+                remote(GS.at[i], GR.at[i], GATE, i, (dp, at_off(i))).wait_recv()
+                to_expert(SB, AR, ACT, i).wait_recv()
+                to_expert(SA, CR, COT, i).wait_send()
+                to_expert(SB, AR, ACT, i).wait_send()
+            gates.append(to_column(GR[i, 0:1, :]))
+        gate = jnp.concatenate(gates, axis=0)
+        GCOL[...] = gate
+        DZ[mine] = (CR[mine].astype(F32) * gate).astype(BF)
+
+        def hidden(q, carry):
+            d = lax.div(q, 2)
+            at = pl.ds(pl.multiple_of(256 * lax.rem(q, 2), 256), 256)
+            to = pl.ds(pl.multiple_of(256 * q, 256), 256)
+            u = dg(AR[mine], WI[d, :, at], 1, 0)
+            dh = dg(CR[mine], WD[d, at, :], 1, 1)
+            phi, slope = normal_parts(u)
+            H[mine, to] = (u * phi).astype(BF)
+            DU[mine, to] = (dh * (phi + slope) * GCOL[...]).astype(BF)
+            return carry
+
+        lax.fori_loop(0, 8, hidden, 0)
+        z = jnp.zeros((2 * cap, D), F32)
+        dx = jnp.zeros((2 * cap, D), F32)
+        for d in range(4):
+            z = z + dg(H[mine, 512 * d:512 * (d + 1)], WD[d], 1, 0)
+            dx = dx + dg(DU[mine, 512 * d:512 * (d + 1)], WI[d], 1, 1)
+        z_low = z.astype(BF).astype(F32)
+        dgate = jnp.sum(CR[mine].astype(F32) * z_low, axis=1, keepdims=True)
+        z_out = (z_low * gate).astype(BF)
+        dx_out = dx.astype(BF)
+        for b, i in enumerate((2 * j, 2 * j + 1)):
+            row = jnp.broadcast_to(to_row(dgate[cap * b:cap * (b + 1)]), (8, cap))
+            if i == 0:
+                DXR[0:cap] = dx_out[:cap]
+                ZR[0:cap] = z_out[:cap]
+                DGR[0] = row
+            else:
+                at = pl.ds(cap * i, cap)
+                SB[at] = dx_out[cap * b:cap * (b + 1)]
+                SA[at] = z_out[cap * b:cap * (b + 1)]
+                DGS[i] = row
+                remote(DGS.at[i], DGR.at[i], DGATE, i, (dp, from_off(i))).start()
+                to_token(SB, DXR, DXE, i).start()
+    for i in range(1, n_e):
+        to_token(SA, ZR, ZED, i).start()
+
+    def wg(d, w):
+        at = pl.ds(pl.multiple_of(512 * d, 512), 512)
+        if w == 0:
+            return dg(AR[...], DU[:, at], 0, 0)
+        return dg(H[:, at], DZ[...], 0, 0)
+
+    yy = lax.div(dp, 2)
+
+    def wgc(jy, w):
+        return remote(WCS.at[2 * jy + w], WCR.at[2 * jy + w], WGC, 2 * jy + w, (dp_c, me))
+
+    def wgy(w):
+        return remote(WYS.at[w], WYR.at[w], WGY, w, (dp_y, me))
+
+    for jy in (1, 0):
+        for w in range(2):
+            WCS[2 * jy + w] = wg(lax.rem(yy + jy, 2) * 2 + 1 - core, w).astype(BF)
+            wgc(jy, w).start()
+    for w in range(2):
+        total = wg(dp_y, w)
+        wgc(1, w).wait_recv()
+        WYS[w] = (total + WCR[2 + w].astype(F32)).astype(BF)
+        wgy(w).start()
+    for w, out in enumerate((grad_in, grad_down)):
+        total = wg(dp, w)
+        wgc(0, w).wait_recv()
+        out[...] = total + WCR[w].astype(F32)
+
+    for i in range(1, n_e):
+        remote(DGS.at[i], DGR.at[i], DGATE, i, (dp, from_off(i))).wait_recv()
+        to_token(SB, DXR, DXE, i).wait_recv()
+    lane_e = iota((T, n_e), 1)
+    dprob = jnp.zeros((T, n_e), F32)
+    for i in range(n_e):
+        got = jnp.sum(jnp.where(lane_cap == SLOT[:, i:i + 1], DGR[i, 0:1, :], 0.0), axis=1, keepdims=True)
+        dprob = jnp.where(lane_e == i, got, dprob)
+    prob = PR[...]
+    dlogit = prob * (dprob - jnp.sum(dprob * prob, axis=1, keepdims=True))
+    high, low = split_two(dlogit)
+    da2 = dg(SELT[...], DXR[...], 1, 0) + dg(high, WR[...], 1, 0) + dg(low, WR[...], 1, 0)
+    g_router = dg(high, A2[...], 0, 0) + dg(low, A2[...], 0, 0)
+    normed, inverse = norm_parts(R[...])
+    back, g_gain2, g_shift2 = norm_back(da2, normed, inverse, NRM[2:3])
+    DR[...] = CP[...].astype(F32) + back
+    dy = DR[...].astype(BF)
+    DO[...] = dg(dy, out_weight(), 1, 0).astype(BF)
+    g_out = dg(dy, O[...], 0, 0).astype(BF)
+
+    def attend_back(g, carry):
+        img = lax.div(g, HEADS // 2)
+        pair = lax.rem(g, HEADS // 2)
+        at = pl.ds(pl.multiple_of(SEQP * img, 16), SEQP)
+        cq = pl.ds(pl.multiple_of(128 * pair, 128), 128)
+        ck = pl.ds(pl.multiple_of(D + 128 * pair, 128), 128)
+        cv = pl.ds(pl.multiple_of(2 * D + 128 * pair, 128), 128)
+        q2, k2, v2, do2 = QKV[at, cq], QKV[at, ck], QKV[at, cv], DO[at, cq]
+        dq = dk = dv = jnp.zeros((SEQP, 128), F32)
+        for hh in range(2):
+            p = PS[2 * g + hh]
+            do_h = do2 * masks[hh]
+            dpr = dg(do_h, v2, 1, 1)
+            ds = (p * (dpr - jnp.sum(dpr * p, axis=1, keepdims=True))).astype(BF)
+            dq = dq + dg(ds, k2 * masks[hh], 1, 0)
+            dk = dk + dg(ds, q2 * masks[hh], 0, 0)
+            dv = dv + dg(p.astype(BF), do_h, 0, 0)
+        DQKV[at, cq] = (dq * HEAD ** -0.5).astype(BF)
+        DQKV[at, ck] = (dk * HEAD ** -0.5).astype(BF)
+        DQKV[at, cv] = dv.astype(BF)
+        return carry
+
+    lax.fori_loop(0, images * HEADS // 2, attend_back, 0)
+
+    for k in range(n_e // 2):
+        g2 = dg(DQKV[:, 2 * part * k:2 * part * (k + 1)], A1[...], 0, 0).astype(BF)
+        for b in range(2):
+            e = 2 * k + b
+            ro = jnp.zeros((1, D), F32)
+            for i in range(n_e):
+                ro = jnp.where(at_off(i) == e, g_router[i:i + 1, :], ro)
+            foot = jnp.where(iota((16, D), 0) == 8, ro, 0.0).astype(BF)
+            for d in range(4):
+                cols = slice(128 * d, 128 * (d + 1))
+                GG[d, brow(e, 0, part), :] = g2[part * b:part * (b + 1), cols]
+                GG[d, brow(e, part, opart), :] = g_out[opart * e:opart * (e + 1), cols]
+                GG[d, brow(e, part + opart, 16), :] = foot[:, cols]
+
+    def rsc(k):
+        d = dp_c if k == 0 else dp_cy
+        return remote(GG.at[d], RCR.at[k], RSC, k, (dp_c, me))
+
+    rsc(1).start()
+    rsc(0).start()
+
+    da1 = jnp.zeros((T, D), F32)
+    for k in range(n_e // 2):
+        da1 = da1 + dg(DQKV[:, 2 * part * k:2 * part * (k + 1)], qkv_weight(k), 1, 0)
+    normed, inverse = norm_parts(XF[...])
+    back, g_gain1, g_shift1 = norm_back(da1, normed, inverse, NRM[0:1])
+    gtok = (DR[...] + back).astype(BF)
+    grad_tok[...] = dg(move, gtok, 0, 0).astype(BF)
+    row8 = iota((8, D), 0)
+    stack = jnp.where(row8 == 0, g_gain1, jnp.where(row8 == 1, g_shift1, jnp.where(row8 == 2, g_gain2, jnp.where(row8 == 3, g_shift2, 0.0))))
+    for k in range(D // 128):
+        SM[0, k, 0:8, :] = stack[:, 128 * k:128 * (k + 1)]
+
+    def smc(k):
+        return remote(SM.at[k], SMCR.at[k], SMC, k, (dp_c if k == 0 else dp_y, me))
+
+    def sm_join(a, b):
+        is_sum = iota(a.shape, len(a.shape) - 2) < 8
+        return jnp.where(is_sum, a + b, jnp.maximum(a, b))
+
+    smc(0).start()
+    rsc(1).wait_recv()
+    RYS[...] = (GG[dp_y].astype(F32) + RCR[1].astype(F32)).astype(BF)
+    rsy = remote(RYS, RYR, RSY, 0, (dp_y, me))
+    rsy.start()
+    smc(0).wait_recv()
+    SM[1] = sm_join(SM[0], SMCR[0])
+    smc(1).start()
+    rsc(0).wait_recv()
+    rsy.wait_recv()
+
+    def rse(i, e):
+        return remote(RES.at[brow(e)], RER.at[i], RSE, i, (dp, at_off(i)))
+
+    def own_sum(e):
+        at = brow(e)
+        return GG[dp, at, :].astype(F32) + RCR[0, at, :].astype(F32) + RYR[at, :].astype(F32)
+
+    for i in range(1, n_e):
+        e = at_off(i)
+        RES[brow(e), :] = own_sum(e).astype(BF)
+        rse(i, e).start()
+    smc(1).wait_recv()
+    SM[2] = sm_join(SM[1], SMCR[1])
+
+    def sme(i):
+        return remote(SM.at[2, lax.div(at_off(i), 2)], SMER.at[i], SME, i, (dp, at_off(i)))
+
+    for i in range(1, n_e):
+        sme(i).start()
+    dense = own_sum(me)
+    for i in range(1, n_e):
+        rse(i, at_off(i)).wait_recv()
+        dense = dense + RER[i].astype(F32)
+    tiny = SM[2, lax.div(me, 2)]
+    for i in range(1, n_e):
+        sme(i).wait_recv()
+        tiny = sm_join(tiny, SMER[i])
+
+    g_qkv = jnp.transpose(dense[0:part])
+    grad_qkv[...] = g_qkv
+    grad_out[...] = jnp.transpose(dense[part:part + opart])
+    grad_router[...] = to_column(dense[part + opart + 8:part + opart + 9])
+    grad_norm[...] = jnp.where(lax.rem(me, 2) == 0, tiny[0:4, 0:HEAD], tiny[0:4, HEAD:128])
+    scale = jnp.sqrt(jnp.minimum(1.0, threshold[0].astype(F32) / tiny[8:16, :]))
+    factors[...] = jnp.sum(jnp.where(iota((8, 128), 0) == iota((8, 128), 1), scale, 0.0), axis=0, keepdims=True)
+    column = me * part + iota((1, part), 1)
+    head = lax.rem(lax.div(column, HEAD), HEADS)
+    scales = jnp.concatenate([scale, scale], axis=1)[:, :part]
+    by_column = jnp.sum(jnp.where(iota((8, part), 0) == head, scales, 0.0), axis=0, keepdims=True)
+    by_column = jnp.where(column < 2 * D, by_column, 1.0)
+    clipped[...] = (w_qkv[...].astype(F32) - LEARN * g_qkv) * by_column
+
+    for w, out in enumerate((grad_in, grad_down)):
+        wgy(w).wait_recv()
+        out[...] = out[...] + WYR[w].astype(F32)
+
+    for i in range(1, n_e):
+        to_token(SA, ZR, ZED, i).wait_recv()
+    total = R[...] + dg(SELT[...], ZR[...], 1, 0)
+    block_out[...] = dg(move, total.astype(BF), 0, 0).astype(BF)
+
+    for i in range(1, n_e):
+        dense_e(i, me, (dp, at_off(i))).wait_send()
+        remote(GS.at[i], GR.at[i], GATE, i, (dp, at_off(i))).wait_send()
+        to_token(SB, DXR, DXE, i).wait_send()
+        to_token(SA, ZR, ZED, i).wait_send()
+        remote(DGS.at[i], DGR.at[i], DGATE, i, (dp, from_off(i))).wait_send()
+        rse(i, at_off(i)).wait_send()
+        sme(i).wait_send()
+    for i in range(n_e):
+        dense_y(i).wait_send()
+    for k in range(2):
+        dense_c(k).wait_send()
+        rsc(k).wait_send()
+        smc(k).wait_send()
+        wgy(k).wait_send()
+        for w in range(2):
+            wgc(k, w).wait_send()
+    for k in range(6):
+        exp_w(k).wait_send()
+    rsy.wait_send()
+
+
+def fused(tokens, w_qkv, w_out, w_router, norm_params, w_in, w_down, routes, threshold, cotangent):
+    rows = tokens.shape[0]
+    n_e = lax.axis_size("expert")
+    images = rows // SEQ
+    T = images * SEQP
+    cap = 15 * routes.shape[1] * rows // (8 * n_e)
+    cap = -(-cap // 16) * 16
+    slots = n_e * cap
+    part, opart = w_qkv.shape[1], w_out.shape[1]
+    drows = w_qkv.shape[0]
+    bundle = part + opart + 16
+    ff = w_in.shape[2]
+    V = pltpu.VMEM
+    spec = pl.BlockSpec(memory_space=pltpu.VMEM)
+    any_spec = pl.BlockSpec(memory_space=pl.ANY)
+    S = jax.ShapeDtypeStruct
+    outs = pl.pallas_call(
+        functools.partial(block_kernel, n_e, cap, rows),
+        out_shape=(
+            S((rows, D), BF), S((rows, D), BF), S((drows, part), F32), S((drows, opart), F32), S((drows, 1), F32),
+            S((4, HEAD), F32), S((D, ff), F32), S((ff, D), F32), S((drows, part), F32), S((1, 128), F32),
+        ),
+        in_specs=[spec] * 7 + [any_spec] * 2 + [pl.BlockSpec(memory_space=pltpu.SMEM)],
+        out_specs=[spec] * 10,
+        scratch_shapes=[
+            V((4, n_e * bundle, 128), BF), V((4, D, ff), BF), V((4, ff, D), BF), V((T, D), F32), V((T, D), BF),
+            V((T, D), F32), V((T, D), BF), V((T, D), BF), V((T, 3 * D), BF), V((T, D), BF),
+            V((images * HEADS, SEQP, SEQP), F32), V((n_e, cap, T), BF), V((T, slots), BF), V((T, n_e), F32),
+            V((16, D), F32), V((T, n_e), F32), V((n_e, D), BF),
+            V((slots, D), BF), V((slots, D), BF), V((slots, D), BF), V((slots, D), BF), V((slots, D), BF), V((slots, D), BF),
+            V((n_e, 8, cap), F32), V((n_e, 8, cap), F32), V((2 * cap, 1), F32), V((n_e, 8, cap), F32), V((n_e, 8, cap), F32),
+            V((slots, 4 * ff), BF), V((slots, 4 * ff), BF), V((slots, D), BF),
+            V((4, D, ff), BF), V((4, D, ff), BF), V((2, D, ff), BF), V((2, D, ff), BF),
+            V((T, 3 * D), BF), V((T, D), BF), V((T, D), F32),
+            V((4, n_e * bundle, 128), BF), V((2, n_e * bundle, 128), BF), V((n_e * bundle, 128), BF),
+            V((n_e * bundle, 128), BF), V((n_e * bundle, 128), BF), V((n_e, bundle, 128), BF),
+            V((3, D // 128, 16, 128), F32), V((2, D // 128, 16, 128), F32), V((n_e, 16, 128), F32),
+            pltpu.SemaphoreType.DMA((17, 8)), pltpu.SemaphoreType.DMA((17, 8)), pltpu.SemaphoreType.DMA((2,)),
+        ],
+        compiler_params=pltpu.CompilerParams(
+            collective_id=0, has_side_effects=True, vmem_limit_bytes=63 * 2 ** 20
+        ),
+    )(
+        tokens, cotangent, routes, w_qkv, w_out, w_router, norm_params,
+        w_in.reshape(D, ff), w_down.reshape(ff, D), threshold,
+    )
+    block_out, grad_tok, grad_qkv, grad_out, grad_router, grad_norm, grad_in, grad_down, clipped, factors = outs
+    return (
+        block_out, grad_tok, grad_qkv, grad_out, grad_router, grad_norm,
+        grad_in[None], grad_down[None], clipped, factors[0, :HEADS],
+    )
 
 
 def layer_norm(values, norm_gain, norm_shift):
@@ -21,7 +600,7 @@
     return (normed * norm_gain + norm_shift, normed, inverse)
 
 
-def norm_back(upstream, normed, inverse, norm_gain):
+def plain_norm_back(upstream, normed, inverse, norm_gain):
     scaled = upstream * norm_gain
     inner_term = (
         scaled
@@ -120,7 +699,11 @@
     gate_weights = jnp.sum(chosen * router_probs[:, None, :], axis=-1)
     flat_routes = routes.reshape(-1)
     onehot = (flat_routes[:, None] == expert_ids[None, :]).astype(jnp.int32)
-    before = jnp.cumsum(onehot, axis=0) - onehot
+    count = flat_routes.shape[0]
+    earlier = jnp.tril(jnp.ones((count, count), jnp.bfloat16), -1)
+    before = jnp.dot(
+        earlier, onehot.astype(jnp.bfloat16), preferred_element_type=jnp.float32
+    ).astype(jnp.int32)
     target_slot = flat_routes * capacity + jnp.sum(before * onehot, axis=1)
     routed = jnp.repeat(second_low, top_count, axis=0)
     outgoing = jnp.zeros((experts * capacity, D), jnp.bfloat16).at[target_slot].set(routed)
@@ -182,7 +765,7 @@
         (((0,), (0,)), ((), ())),
         precision=lax.Precision.HIGHEST,
     )
-    grad_resid_two, gain_two_grad, shift_two_grad = norm_back(
+    grad_resid_two, gain_two_grad, shift_two_grad = plain_norm_back(
         grad_second, normed_two, inverse_two, gain_rows[2]
     )
     grad_resid = upstream + grad_resid_two
@@ -217,7 +800,7 @@
     )
     grad_qkv = contract_rows(first_low, grad_qkv_rows)
     grad_first = contract_cols(grad_qkv_rows, back_qkv)
-    grad_source, gain_one_grad, shift_one_grad = norm_back(
+    grad_source, gain_one_grad, shift_one_grad = plain_norm_back(
         grad_first, normed_one, inverse_one, gain_rows[0]
     )
     grad_tokens = (grad_resid + grad_source).astype(jnp.bfloat16)
@@ -307,4 +890,5 @@
         P("dp", "expert"),
         P(),
     )
-    return jax.shard_map(shards, mesh=mesh, in_specs=in_specs, out_specs=out_specs, check_vma=False)
+    fits = mesh.shape["dp"] == 4 and mesh.shape["expert"] == 8
+    return jax.shard_map(fused if fits else shards, mesh=mesh, in_specs=in_specs, out_specs=out_specs, check_vma=False)

time: 825 us -> 228 us (0.28); the launches traced: 813 us -> 227 us
  blocking collectives: 327 us -> 0 us
  waiting for transfers between devices: 225 us -> 0 us
  Pallas kernels: 0 us -> 210 us
  matrix products: 108 us -> 0 us
  local copies, waits for them, and re-layouts: 73.7 us -> 16 us
  other arithmetic: 40.2 us -> 0 us
  starting transfers between devices: 23.3 us -> 0 us
  between operations: 16 us -> 1.34 us
    all_gather x11 -> x0, blocking collectives: 263 us -> none  [the longest x1 57.9 us: fetch_backward(): lax.all_gather(w_qkv, 'expert', axis=1, tiled=True)]
    pallas_call x0 -> x1, Pallas kernels: none -> 210 us  [fused(): pl.pallas_call(functools.partial(block_kernel, n_e, cap, rows), out_shape...]
    unnamed x18 -> x0, waiting for transfers between devices: 118 us -> none
    dot_general x21 -> x0, matrix products: 108 us -> none  [the longest x1 31 us: shards(): hidden = jnp.dot(arrived, full_in[0], preferred_element_type=jnp.float32)]
    reduce_scatter x4 -> x0, waiting for transfers between devices: 94.8 us -> none  [the longest x1 32.4 us: shards(): lax.psum_scatter(grad_down[None].astype(jnp.bfloat16), 'dp', scatter_dime...]
    pmax x1 -> x0, blocking collectives: 40.2 us -> none  [shards(): peak_logit = lax.pmax(head_peaks, ('dp', 'expert'))]
    all_to_all x4 -> x0, starting transfers between devices: 22.5 us -> none  [the longest x1 7.37 us: shards(): lax.all_to_all(back_slots.reshape(experts, capacity, D), 'expert', split_...]
    unnamed x1 -> x0, blocking collectives: 17.6 us -> none
  transfers between devices with their start and end apart: 18 -> 0, of which waited for: 9 -> 0; matrix products, arithmetic and copies ran while one was open for 27% -> 0% of each run, Pallas kernels for 0% -> 0%
where the time goes in v1:
time: 228 us; the launch traced here: 227 us
  Pallas kernels  210 us (92%)
  local copies, waits for them, and re-layouts  16 us (7%)
    pallas_call x1, Pallas kernels, fused(): pl.pallas_call(functools.partial(block_kernel, n_e, cap, rows), out_shape...  210 us
    unnamed x29, local copies, waits for them, and re-layouts  14.9 us

profile of v1, /device:TPU:0, one launch (start us, length us, event | category | flops | bytes accessed | tf_op | source)
XLA Modules:
  0.0 227.2 jit_solution(9361609741771018135)
XLA Ops:
  0.6 0.0 copy-start.4
  1.3 0.0 copy-start.7
  1.3 1.4 copy.22.w_out
  2.8 0.0 copy-done.7
  2.8 0.7 copy.23.w_router
  3.5 0.0 copy-done.4
  3.5 0.0 copy-start.5
  3.5 0.7 copy.21.w_qkv
  4.2 0.0 copy-done.5
  4.2 0.8 copy.20.routes
  5.1 209.8 %shard_map.177 = (bf16[394,512]{1,0:T(8,128)(2,1)}, bf16[394,512]{1,0:T(8,128)(2,1)}, f32[128,192]{1,0:T(8,128)}, f32[128,64]{1,0:T(8,128)}, f32[128,1]{1,0:T(8,...) custom-call(bf16[394,512]{1,0:T(8,128)(2,1)} %tok.1, ...), custom_call_target="tpu_custom_call" | custom-call | tf_op jit(solution)/shard_map/pallas_call | solution.py:558
  214.9 0.0 copy-start.3
  214.9 1.5 copy.26
  216.4 1.1 slice_bitcast_fusion
  217.5 0.0 copy-start.2
  217.5 1.6 copy.25
  219.1 0.0 copy-start.1
  219.1 1.7 copy.24
  220.8 1.6 copy.27
  222.5 0.0 copy-done.3
  222.5 0.8 copy.34
  223.2 0.0 copy-done.2
  223.2 0.0 copy-start.6
  223.2 0.8 copy.35
  224.0 0.0 copy-done.6
  224.0 0.6 copy.36
  224.6 0.0 copy-done.1
  224.6 0.0 copy-start
  224.6 1.0 copy.37
  225.6 0.6 copy-done
  226.2 1.0 copy.38
Async XLA Ops:
  0.6 2.9 %copy-start.4 = (bf16[128,192]{0,1:T(8,128)(2,1)S(1)}, bf16[128,192]{0,1:T(8,128)(2,1)}, u32[]{:S(2)}) copy-start(bf16[128,192]{0,1:T(8,128)(2,1)} %param.11) | copy-start | bytes 147460
  1.3 1.5 copy-start.7
  3.5 0.7 copy-start.5
  214.9 7.6 %copy-start.3 = (bf16[394,512]{1,0:T(8,128)(2,1)S(1)}, bf16[394,512]{1,0:T(8,128)(2,1)}, u32[]{:S(2)}) copy-start(bf16[394,512]{1,0:T(8,128)(2,1)} %get-tuple-element.50) | copy-start | bytes 1210372
  217.5 5.7 %copy-start.2 = (bf16[394,512]{1,0:T(8,128)(2,1)S(1)}, bf16[394,512]{1,0:T(8,128)(2,1)}, u32[]{:S(2)}) copy-start(bf16[394,512]{1,0:T(8,128)(2,1)} %get-tuple-element.51) | copy-start | bytes 1210372
  219.1 5.5 %copy-start.1 = (f32[512,512]{1,0:T(8,128)S(1)}, f32[512,512]{1,0:T(8,128)}, u32[]{:S(2)}) copy-start(f32[512,512]{1,0:T(8,128)} %get-tuple-element.26) | copy-start | bytes 3145732
  223.2 0.8 copy-start.6
  224.6 1.6 copy-start
